TPU v7x, 32 devices: a whole 2x2x4 slice. The times are simulated.
32 devices in a mesh: req: 16 (over z, y, x), mlp: 2 (over core).
Axes of the slice: x: 2, y: 2, z: 4, core: 2. Of those that a mesh axis runs over, the one named last changes fastest.
Arguments:
- resid: bfloat16 [512, 2048], P('req'), may hold values from -50 to 50
- q_in: bfloat16 [512, 2048], P('req', 'mlp'), may hold values from -36 to 36
- kv_in: bfloat16 [512, 2, 512], P('req', None, 'mlp'), may hold values from -36 to 36
- parents: int32 [32, 16], P('req'), may hold values from -1 to 14, as said below
- counts: int32 [32], P('req'), may hold values from 8 to 16, as said below
- accept_leaf: int32 [32], P('req'), may hold values from 0 to 15, as said below
- cache: bfloat16 [1024, 2, 128, 512], P('req', None, None, 'mlp'), may hold values from -6 to 6
- held_table: int32 [32, 48], P('req'), may hold values from 0 to 63, as said below
- held_len: int32 [32], P('req'), may hold values from 1 to 6144, as said below
- prev_owner: int32 [16], P('req'), may hold values from 0 to 15, as said below
- w_out: bfloat16 [2048, 2048], P('mlp'), may hold values from -0.125 to 0.125
- gain_mid: bfloat16 [2048], replicated, may hold values from 0.099609375 to 1.8984375
- w_in: bfloat16 [2, 8192, 2048], P(None, ('req', 'mlp')), may hold values from -0.125 to 0.125
- w_down: bfloat16 [8192, 2048], P(('req', 'mlp')), may hold values from -0.0625 to 0.0625
- gain_next: bfloat16 [2048], replicated, may hold values from 0.099609375 to 1.8984375
- w_next: bfloat16 [2048, 3072], P(None, 'mlp'), may hold values from -0.125 to 0.125
Outputs:
- hidden_out: bfloat16 [512, 2048], P('req')
- next_qkv: bfloat16 [512, 3072], P('req', 'mlp')
- accepted_kv: bfloat16 [512, 2, 512], P('req', None, 'mlp')
Inputs may be any that keep to these rules, and one draw needn't show every extreme that they name: parents[r, 0] is -1; for i of 1 or more parents[r, i] lies in 0 to i - 1. Draft tokens 0 to counts[r] - 1 of request r are live; some request has 16. `accept_leaf`: a live draft token of the request. `held_len`: entry 2 d holds the length of request 2 d, entry 2 d + 1 that of request 2 e + 1 where prev_owner[e] = d; some entry is 6144; the pages used by the two caches of one index of req are distinct. `held_table`: rows 2 d and 2 d + 1 belong to index d of req, as in held_len. `prev_owner`: one cycle through all indices of req, so never d itself.
All inputs are finite; a program needn't handle non-finite values.
Results may differ from a plain program's by a relative error of at most 0.014.
Values may be sent and summed in bfloat16 or wider, within the bound.
A program may use at most 128 MiB of HBM per device.

v0:
```python
import math

import jax
import jax.numpy as jnp
from jax import lax
from jax.sharding import PartitionSpec as P

HEAD_DIM = 64
GROUP = 4


norm_eps = 1e-05
masked_score = -1e30


def ancestors(parents):
    count_nodes = parents.shape[-1]
    nodes = jnp.arange(count_nodes, dtype=jnp.int32)
    reach = (parents[..., :, None] == nodes).astype(jnp.float32) + jnp.eye(
        count_nodes, dtype=jnp.float32
    )
    for step in range(count_nodes.bit_length()):
        reach = jnp.minimum(
            jnp.einsum("sij,sjk->sik", reach, reach, precision=lax.Precision.HIGHEST), 1.0
        )
    return reach


def rms_scale(rows, gain):
    values = rows.astype(jnp.float32)
    factor = lax.rsqrt(jnp.mean(values * values, axis=-1, keepdims=True) + norm_eps)
    return (values * factor * gain.astype(jnp.float32)).astype(jnp.bfloat16)


def swiglu_rows(rows, w_in, w_down):
    dims = (((1,), (1,)), ((), ()))
    gate = lax.dot_general(rows, w_in[0], dims, preferred_element_type=jnp.float32)
    up_part = lax.dot_general(rows, w_in[1], dims, preferred_element_type=jnp.float32)
    hidden = (jax.nn.silu(gate) * up_part).astype(jnp.bfloat16)
    return jnp.dot(hidden, w_down, preferred_element_type=jnp.float32)


def compact_path(reach, leaves, rows):
    count_nodes = reach.shape[-1]
    nodes = jnp.arange(count_nodes, dtype=jnp.int32)
    leaf_hot = (nodes[None, :] == leaves[:, None]).astype(jnp.float32)
    path = jnp.einsum("si,sij->sj", leaf_hot, reach, precision=lax.Precision.HIGHEST)
    ranks = jnp.cumsum(path, axis=1) - path
    places = nodes.astype(jnp.float32)
    select = path[:, None, :] * (ranks[:, None, :] == places[None, :, None]).astype(jnp.float32)
    return jnp.einsum(
        "spj,sjw->spw", select.astype(jnp.bfloat16), rows, preferred_element_type=jnp.float32
    ).astype(jnp.bfloat16)


def per_device(
    resid,
    q_in,
    kv_in,
    parents,
    counts,
    accept_leaf,
    cache,
    held_table,
    held_len,
    prev_owner,
    w_out,
    gain_mid,
    w_in,
    w_down,
    gain_next,
    w_next,
):
    tree_len = parents.shape[1]
    kv_width = kv_in.shape[2]
    kv_local = kv_width // HEAD_DIM
    scale = HEAD_DIM ** (-0.5)
    queries = q_in.reshape(2, tree_len, kv_local, GROUP, HEAD_DIM)
    every_query = lax.all_gather(q_in[tree_len:], "req", axis=0, tiled=True)
    owner_list = lax.all_gather(prev_owner, "req", axis=0, tiled=True)
    device_id = lax.axis_index("req")
    senders = jnp.arange(owner_list.shape[0], dtype=jnp.int32)
    sender = jnp.sum(jnp.where(owner_list == device_id, senders, 0))
    foreign = lax.dynamic_slice_in_dim(every_query, sender * tree_len, tree_len, 0)
    held_queries = jnp.stack([q_in[:tree_len], foreign]).reshape(
        2, tree_len, kv_local, GROUP, HEAD_DIM
    )
    page_len = cache.shape[2]
    block_pages = math.gcd(held_table.shape[1], max(1, 1024 // page_len))
    block_keys = block_pages * page_len
    num_blocks = held_table.shape[1] // block_pages
    positions = jnp.arange(block_keys, dtype=jnp.int32)

    def attend_block(block, state):
        running, total, accum = state
        page_ids = lax.dynamic_slice_in_dim(held_table, block * block_pages, block_pages, 1)
        gathered = cache[page_ids]
        key_rows = gathered[:, :, 0].reshape(2, block_keys, kv_local, HEAD_DIM)
        value_rows = gathered[:, :, 1].reshape(2, block_keys, kv_local, HEAD_DIM)
        scores = (
            jnp.einsum(
                "sqghe,skge->sghqk", held_queries, key_rows, preferred_element_type=jnp.float32
            )
            * scale
        )
        visible = (block * block_keys + positions)[None, :] < held_len[:, None]
        visible = visible[:, None, None, None, :]
        scores = jnp.where(visible, scores, masked_score)
        newest = jnp.maximum(running, jnp.max(scores, axis=-1))
        weights = jnp.where(visible, jnp.exp(scores - newest[..., None]), 0.0)
        factor = jnp.exp(running - newest)
        total = total * factor + jnp.sum(weights, axis=-1)
        update = jnp.einsum(
            "sghqk,skge->sghqe",
            weights,
            value_rows.astype(jnp.float32),
            precision=lax.Precision.HIGHEST,
        )
        accum = accum * factor[..., None] + update
        return (newest, total, accum)

    stat_shape = (2, kv_local, GROUP, tree_len)
    start_state = (
        jnp.full(stat_shape, masked_score, jnp.float32),
        jnp.zeros(stat_shape, jnp.float32),
        jnp.zeros(stat_shape + (HEAD_DIM,), jnp.float32),
    )
    running, total, accum = lax.fori_loop(0, num_blocks, attend_block, start_state)
    cache_out = accum / total[..., None]
    sent_out = jnp.transpose(cache_out[1], (2, 0, 1, 3)).reshape(
        tree_len, kv_local * GROUP * HEAD_DIM
    )
    sent_max = jnp.transpose(running[1], (2, 0, 1)).reshape(tree_len, kv_local * GROUP)
    sent_total = jnp.transpose(total[1], (2, 0, 1)).reshape(tree_len, kv_local * GROUP)
    back_out, back_max, back_total = (
        lax.all_gather(sent_out.astype(jnp.bfloat16), "req", axis=0, tiled=True).astype(
            sent_out.dtype
        ),
        lax.all_gather(sent_max.astype(jnp.bfloat16), "req", axis=0, tiled=True).astype(
            sent_max.dtype
        ),
        lax.all_gather(sent_total.astype(jnp.bfloat16), "req", axis=0, tiled=True).astype(
            sent_total.dtype
        ),
    )
    first_row = prev_owner[0] * tree_len
    recv_out = lax.dynamic_slice_in_dim(back_out, first_row, tree_len, 0).reshape(
        tree_len, kv_local, GROUP, HEAD_DIM
    )
    recv_max = lax.dynamic_slice_in_dim(back_max, first_row, tree_len, 0).reshape(
        tree_len, kv_local, GROUP
    )
    recv_total = lax.dynamic_slice_in_dim(back_total, first_row, tree_len, 0).reshape(
        tree_len, kv_local, GROUP
    )
    part_out = jnp.stack([cache_out[0], jnp.transpose(recv_out, (1, 2, 0, 3))])
    part_max = jnp.stack([running[0], jnp.transpose(recv_max, (1, 2, 0))])
    part_total = jnp.stack([total[0], jnp.transpose(recv_total, (1, 2, 0))])
    reach = ancestors(parents)
    live = jnp.arange(tree_len, dtype=jnp.int32)[None, :] < counts[:, None]
    allowed = ((reach > 0.5) & live[:, None, :])[:, None, None, :, :]
    draft_keys = kv_in[:, 0].reshape(2, tree_len, kv_local, HEAD_DIM)
    draft_values = kv_in[:, 1].reshape(2, tree_len, kv_local, HEAD_DIM)
    tree_scores = (
        jnp.einsum("sqghe,skge->sghqk", queries, draft_keys, preferred_element_type=jnp.float32)
        * scale
    )
    tree_scores = jnp.where(allowed, tree_scores, masked_score)
    tree_max = jnp.max(tree_scores, axis=-1)
    tree_weights = jnp.where(allowed, jnp.exp(tree_scores - tree_max[..., None]), 0.0)
    tree_total = jnp.sum(tree_weights, axis=-1)
    tree_accum = jnp.einsum(
        "sghqk,skge->sghqe",
        tree_weights,
        draft_values.astype(jnp.float32),
        precision=lax.Precision.HIGHEST,
    )
    overall = jnp.maximum(part_max, tree_max)
    cache_weight = part_total * jnp.exp(part_max - overall)
    tree_weight = jnp.exp(tree_max - overall)
    merged = (part_out * cache_weight[..., None] + tree_accum * tree_weight[..., None]) / (
        cache_weight + tree_total * tree_weight
    )[..., None]
    attended = (
        jnp.transpose(merged, (0, 3, 1, 2, 4))
        .reshape(2 * tree_len, kv_local * GROUP * HEAD_DIM)
        .astype(jnp.bfloat16)
    )
    partial_proj = jnp.dot(attended, w_out, preferred_element_type=jnp.float32)
    projected = lax.psum(partial_proj, "mlp")
    mixed = (resid.astype(jnp.float32) + projected).astype(jnp.bfloat16)
    normed = rms_scale(mixed, gain_mid)
    column = lax.axis_index("mlp")
    half_count = normed.shape[0] // lax.axis_size("mlp")
    every_row = lax.all_gather(normed, "req", axis=0, tiled=True)
    mlp_half = lax.psum_scatter(
        swiglu_rows(every_row, w_in, w_down), ("req", "mlp"), scatter_dimension=0, tiled=True
    )
    base_half = lax.dynamic_slice_in_dim(mixed, column * half_count, half_count, 0)
    out_half = (base_half.astype(jnp.float32) + mlp_half).astype(jnp.bfloat16)
    hidden_out = lax.all_gather(out_half, "mlp", axis=0, tiled=True)
    next_normed = rms_scale(hidden_out, gain_next)
    next_qkv = jnp.dot(next_normed, w_next, preferred_element_type=jnp.float32).astype(jnp.bfloat16)
    accepted = compact_path(reach, accept_leaf, kv_in.reshape(2, tree_len, 2 * kv_width))
    accepted_kv = accepted.reshape(2 * tree_len, 2, kv_width)
    return (hidden_out, next_qkv, accepted_kv)


def solution(mesh):
    placed = (
        P("req", None),
        P("req", "mlp"),
        P("req", None, "mlp"),
        P("req", None),
        P("req"),
        P("req"),
        P("req", None, None, "mlp"),
        P("req", None),
        P("req"),
        P("req"),
        P("mlp", None),
        P(),
        P(None, ("req", "mlp"), None),
        P(("req", "mlp"), None),
        P(),
        P(None, "mlp"),
    )
    return jax.shard_map(
        per_device,
        mesh=mesh,
        in_specs=placed,
        out_specs=(P("req", None), P("req", "mlp"), P("req", None, "mlp")),
        check_vma=False,
    )
```

profile of v0, /device:TPU:0, one launch (start us, length us, event | category | flops | bytes accessed | tf_op | source)
XLA Modules:
  0.0 556.2 jit_solution(9332401869798486938)
XLA Ops:
  10.0 16.2 %all-reduce = s32[16]{0:T(128)S(1)} all-reduce(s32[16]{0:T(128)S(1)} %dynamic-update-slice), channel_id=1, replica_groups=mesh['req'=16,'mlp'=2] {'req'}, use_global_device_ids=true, to_apply=%add | all-reduce | flops 16 | bytes 128
  28.2 40.2 %all_gather.21 = bf16[256,1024]{1,0:T(8,128)(2,1)S(1)} all-gather(bf16[16,1024]{1,0:T(8,128)(2,1)S(1)} %get-tuple-element.245), channel_id=1, replica_groups=mesh['req'=16,'mlp'=2] {'req'}, dimensions={0}, use_global_device_ids=true | all-gather | bytes 557056 | tf_op jit(solution)/shard_map/all_gather | solution.py:79
  68.9 121.3 %while.18 = (s32[]{:T(128)}, f32[2,4,4,16]{3,2,1,0:T(4,128)S(1)}, f32[2,4,4,16]{3,2,1,0:T(4,128)S(1)}, f32[2,4,4,16,64]{4,3,2,1,0:T(8,128)}, s32[2]{0:T(128)}, /...) while((s32[]{:T(128)}, f32[2,4,4,16]{3,2,1,0:T(4,128)S(1)}, ...), condition=%wide.region_4.5_spmd.clone, body=%wide.region_1.4_spmd.clone.sunk | while | flops 476158528 | bytes 25547404 | solution.py:128
  69.8 4.1 gather_fusion
  75.4 1.7 copy.94
  78.5 1.7 bitcast_reduce_fusion.2
  80.9 2.5 copy.95
  83.3 2.3 reshape.267
  85.7 3.5 fusion.115
  90.0 4.1 gather_fusion
  95.5 1.7 copy.94
  98.7 1.7 bitcast_reduce_fusion.2
  101.1 2.5 copy.95
  103.5 2.3 reshape.267
  105.8 3.5 fusion.115
  110.2 4.1 gather_fusion
  115.8 1.7 copy.94
  118.9 1.7 bitcast_reduce_fusion.2
  121.3 2.5 copy.95
  123.7 2.3 reshape.267
  126.1 3.5 fusion.115
  130.4 4.1 gather_fusion
  136.0 1.7 copy.94
  139.1 1.7 bitcast_reduce_fusion.2
  141.5 2.5 copy.95
  144.0 2.3 reshape.267
  146.3 3.5 fusion.115
  150.6 4.1 gather_fusion
  159.3 1.7 bitcast_reduce_fusion.2
  161.7 2.5 copy.95
  164.2 2.3 reshape.267
  166.5 3.5 fusion.115
  170.9 4.1 gather_fusion
  179.5 1.7 bitcast_reduce_fusion.2
  181.9 2.5 copy.95
  184.4 2.3 reshape.267
  186.7 3.5 fusion.115
  191.7 36.1 %all_gather.24 = bf16[256,16]{1,0:T(8,128)(2,1)S(1)} all-gather(bf16[16,16]{1,0:T(8,128)(2,1)S(1)} %copy.53), channel_id=1, replica_groups=mesh['req'=16,'mlp'=2] {'req'}, dimensions={0}, use_global_device_ids=true | all-gather | bytes 8704 | tf_op jit(solution)/shard_map/all_gather | solution.py:142
  227.8 37.6 %all_gather.25 = bf16[256,16]{1,0:T(8,128)(2,1)S(1)} all-gather(bf16[16,16]{1,0:T(8,128)(2,1)S(1)} %copy.55), channel_id=1, replica_groups=mesh['req'=16,'mlp'=2] {'req'}, dimensions={0}, use_global_device_ids=true | all-gather | bytes 8704 | tf_op jit(solution)/shard_map/all_gather | solution.py:139
  267.0 38.5 %all_gather.23 = bf16[256,1024]{1,0:T(8,128)(2,1)S(1)} all-gather(bf16[16,1024]{1,0:T(8,128)(2,1)S(1)} %convert_element_type.116), channel_id=1, replica_groups=mesh['req'=16,'mlp'=2] {'req'}, dimensions={0}, use_global_device_ids=true | all-gather | bytes 557056 | tf_op jit(solution)/shard_map/all_gather | solution.py:136
  307.2 3.8 fusion.84
  311.0 15.9 %all-reduce.3.cloned.1.call-done = f32[32,2048]{1,0:T(8,128)} async-done(((f32[32,2048]{1,0:T(8,128)}), f32[32,2048]{1,0:T(8,128)}) %all-reduce.3.cloned.1.call-update) | async-done | bytes 262160 | tf_op jit(solution)/shard_map/psum | solution.py:190
  328.8 63.7 %all-gather.2.cloned.1.call-done = bf16[512,2048]{1,0:T(8,128)(2,1)} async-done(((bf16[32,2048]{1,0:T(8,128)(2,1)}), bf16[512,2048]{1,0:T(8,128)(2,1)}) %all-gather.2.cloned.1.call-update) | async-done | bytes 2097168 | tf_op jit(solution)/shard_map/all_gather | solution.py:195
  392.5 3.5 fusion.33
  396.1 5.6 %fusion.28 = f32[512,2048]{1,0:T(8,128)} fusion(bf16[256,2048]{1,0:T(8,128)(2,1)S(1)} %copy-done, bf16[512,2048]{1,0:T(8,128)(2,1)S(1)} %copy-done.1, bf16[2,256,2048]{2,1,0:T(8,128)(2,1)} %param.30, f32[512,256]{1,0:T(8,128)} %fusion.33), kind=kOutput, calls=%fused_computation.40 | convolution fusion | flops 1074528256 | bytes 8912896 | tf_op jit(solution)/shard_map/dot_general | solution.py:40
  403.6 137.8 %reduce-scatter.2.cloned.1.call-done = f32[16,2048]{1,0:T(8,128)} async-done(((f32[512,2048]{1,0:T(8,128)}), f32[16,2048]{1,0:T(8,128)}) %reduce-scatter.2.cloned.1.call-update) | async-done | bytes 131088 | tf_op jit(solution)/shard_map/reduce_scatter | solution.py:196
  542.3 1.9 all_gather.27
  544.3 4.7 convolution_convert_fusion
  (173 shorter events, 43.7 us)
Async XLA Ops:
  7.2 388.9 %copy-start = (bf16[256,2048]{1,0:T(8,128)(2,1)S(1)}, bf16[256,2048]{1,0:T(8,128)(2,1)}, u32[]{:S(2)}) copy-start(bf16[256,2048]{1,0:T(8,128)(2,1)} %param.31) | copy-start | bytes 3145732
  7.2 319.7 %all-reduce.3.cloned.1.call-start = ((), (), s32[]{:S(2)}) async-start(), calls=%async_computation.1 | async-start | bytes 524288 | tf_op jit(solution)/shard_map/psum | solution.py:190
  68.9 121.4 %copy-start.3 = (bf16[32,1024]{1,0:T(8,128)(2,1)S(1)}, bf16[32,1024]{1,0:T(8,128)(2,1)}, u32[]{:S(2)}) copy-start(bf16[32,1024]{1,0:T(8,128)(2,1)} %param.19) | copy-start | bytes 196612
  68.9 196.8 %copy-start.8 = (s32[2,16]{1,0:T(2,128)S(1)}, s32[2,16]{1,0:T(2,128)}, u32[]{:S(2)}) copy-start(s32[2,16]{1,0:T(2,128)} %param.21) | copy-start | bytes 388
  68.9 197.4 %copy-start.9 = (s32[2]{0:T(128)S(1)}, s32[2]{0:T(128)}, u32[]{:S(2)}) copy-start(s32[2]{0:T(128)} %param.22) | copy-start | bytes 28
  68.9 197.7 %copy-start.2 = (bf16[32,2,256]{2,1,0:T(2,128)(2,1)S(1)}, bf16[32,2,256]{2,1,0:T(2,128)(2,1)}, u32[]{:S(2)}) copy-start(bf16[32,2,256]{2,1,0:T(2,128)(2,1)} %param.20) | copy-start | bytes 98308
  75.4 3.0 copy-start.5
  95.5 3.0 copy-start.5
  115.8 3.0 copy-start.5
  136.0 3.0 copy-start.5
  156.2 3.0 copy-start.5
  176.4 3.0 copy-start.5
  307.1 3.9 copy-start.6
  307.1 19.7 %copy-start.4 = (bf16[32,2048]{1,0:T(8,128)(2,1)S(1)}, bf16[32,2048]{1,0:T(8,128)(2,1)}, u32[]{:S(2)}) copy-start(bf16[32,2048]{1,0:T(8,128)(2,1)} %param.18) | copy-start | bytes 393220
  310.9 81.6 %all-gather.2.cloned.1.call-start = ((), (), s32[]{:S(2)}) async-start(), calls=%async_computation.2 | async-start | bytes 2228224 | tf_op jit(solution)/shard_map/all_gather | solution.py:195
  328.8 212.6 %reduce-scatter.2.cloned.1.call-start = ((), (), s32[]{:S(2)}) async-start(), calls=%async_computation.3 | async-start | bytes 4325376 | tf_op jit(solution)/shard_map/reduce_scatter | solution.py:196
  392.5 3.6 copy-start.1
  401.7 0.7 copy-start.7
  401.7 0.7 copy-start.10
Sparse Core Ops, SparseCore 0:
  311.1 15.7 all-reduce.2
  330.6 61.8 all-gather.1
  401.8 139.4 reduce-scatter.1
where the time goes:
time: 558 us; the launch traced here: 556 us
  waiting for transfers between devices  217 us (39%)
  blocking collectives  171 us (31%)
  local copies, waits for them, and re-layouts  87 us (16%)
  matrix products  51.2 us (9%)
  between operations  15.4 us (3%)
  other arithmetic  14.3 us (3%)
    reduce_scatter x1, waiting for transfers between devices, per_device(): lax.psum_scatter(swiglu_rows(every_row, w_in, w_down), ('req', 'mlp'), sc...  138 us
    all_gather x1, waiting for transfers between devices, per_device(): every_row = lax.all_gather(normed, 'req', axis=0, tiled=True)  63.7 us
    all_gather x1, blocking collectives, per_device(): every_query = lax.all_gather(q_in[tree_len:], 'req', axis=0, tiled=True)  40.2 us
    all_gather x1, blocking collectives, per_device(): lax.all_gather(sent_out.astype(jnp.bfloat16), 'req', axis=0, tiled=True)  38.5 us
    all_gather x1, blocking collectives, per_device(): lax.all_gather(sent_max.astype(jnp.bfloat16), 'req', axis=0, tiled=True)  37.6 us
    all_gather x1, blocking collectives, per_device(): lax.all_gather(sent_total.astype(jnp.bfloat16), 'req', axis=0, tiled=True)  36.1 us
    while x30, local copies, waits for them, and re-layouts  25.1 us
    gather x6, local copies, waits for them, and re-layouts, attend_block(): gathered = cache[page_ids]  24.4 us
  transfers between devices with their start and end apart: 3, of which 3 were waited for; matrix products, arithmetic and copies ran while one was open for 0% of the time, Pallas kernels for 0%

commit v1 on v0

v1 whole, which is shorter than its diff:
```python
import functools

import jax
import jax.numpy as jnp
from jax import lax
from jax.experimental import pallas as pl
from jax.experimental.pallas import tpu as pltpu
from jax.sharding import PartitionSpec as P

HEAD_DIM = 64
GROUP = 4
EPS = 1e-05
MESH = pl.DeviceIdType.MESH
F32 = jnp.float32
BF16 = jnp.bfloat16
VMEM = pltpu.VMEM
OWNER_LANE = 65
COUNT_LANE = 64


def layout(n):
    depth = 4 if n % 4 == 0 else 1
    return depth, n // depth


def position(n):
    depth, plane = layout(n)
    me = lax.axis_index("req")
    return me, me // plane, lax.rem(me, plane), lax.axis_index("mlp")


def greet(n, partner):
    depth, plane = layout(n)
    me, z, p, c = position(n)
    barrier = pltpu.get_barrier_semaphore()
    peers = [(lax.rem(z + k, depth) * plane + p, c) for k in range(1, depth)]
    peers += [(z * plane + lax.rem(p + k, plane), c) for k in range(1, plane)]
    if partner:
        peers.append((me, 1 - c))
    for peer in peers:
        pl.semaphore_signal(barrier, inc=1, device_id=peer, device_id_type=MESH)
    pl.semaphore_wait(barrier, len(peers))


def line_copies(n, ref, send_sem, recv_sem):
    depth, plane = layout(n)
    me, z, p, c = position(n)
    made = []
    for k in range(1, depth):
        made.append(
            pltpu.make_async_remote_copy(
                ref.at[me],
                ref.at[me],
                send_sem.at[k - 1],
                recv_sem.at[k - 1],
                device_id=(lax.rem(z + k, depth) * plane + p, c),
                device_id_type=MESH,
            )
        )
    return made


def plane_copies(n, ref, back, send_sem, recv_sem):
    depth, plane = layout(n)
    me, z, p, c = position(n)
    block = lax.rem(z - back + depth, depth) * plane + p
    made = []
    for k in range(1, plane):
        made.append(
            pltpu.make_async_remote_copy(
                ref.at[block],
                ref.at[block],
                send_sem.at[depth - 1 + back * (plane - 1) + k - 1],
                recv_sem.at[depth - 1 + back * (plane - 1) + k - 1],
                device_id=(z * plane + lax.rem(p + k, plane), c),
                device_id_type=MESH,
            )
        )
    return made


def parent_matrix(parents_ref, r):
    size = parents_ref.shape[1]
    row = lax.broadcasted_iota(jnp.int32, (size, 128), 0)
    lane = lax.broadcasted_iota(jnp.int32, (size, 128), 1)
    hot = jnp.zeros((size, 128), F32)
    for i in range(size):
        hot = jnp.where((row == i) & (lane == parents_ref[r, i]), 1.0, hot)
    return hot


def share_kernel(
    n, parents_ref, counts_ref, owner_ref, q_ref, kv_ref, resid_ref,
    out_ref, owners_ref, blocks, send_sem, recv_sem,
):
    depth, plane = layout(n)
    me, z, p, c = position(n)
    rows = out_ref.shape[0]
    qw, kw, half = q_ref.shape[1], kv_ref.shape[1], resid_ref.shape[1] // 2
    tail = qw + kw + half
    lane = lax.broadcasted_iota(jnp.int32, (rows, 128), 1)
    info = parent_matrix(parents_ref, 1)
    info = jnp.where(lane == COUNT_LANE, counts_ref[1].astype(F32), info)
    info = jnp.where(lane == OWNER_LANE, owner_ref[0].astype(F32), info)
    blocks[me, :, :qw] = q_ref[rows:, :]
    blocks[me, :, qw : qw + kw] = kv_ref[rows:, :]
    blocks[me, :, qw + kw : tail] = resid_ref[rows:, pl.ds(pl.multiple_of(c * half, 128), half)]
    blocks[me, :, tail:] = info.astype(BF16)
    greet(n, False)
    line = line_copies(n, blocks, send_sem, recv_sem)
    for copy in line:
        copy.start()
    started = list(line)
    for back in range(depth):
        if back:
            line[back - 1].wait_recv()
        made = plane_copies(n, blocks, back, send_sem, recv_sem)
        for copy in made:
            copy.start()
        started += made
    for copy in started[depth - 1 :]:
        copy.wait_recv()
    for copy in started:
        copy.wait_send()

    out_ref[...] = jnp.zeros_like(out_ref)

    def pick(j, carry):
        tags = blocks[j, :, tail:].astype(F32)
        owner = jnp.sum(jnp.where(lane == OWNER_LANE, tags, 0.0), axis=1, keepdims=True)
        owners_ref[j] = jnp.broadcast_to(owner, (rows, 128))[:8].astype(jnp.int32)
        mine = (owner == me.astype(F32)).astype(F32)
        out_ref[...] = (out_ref[...].astype(F32) + blocks[j].astype(F32) * mine).astype(BF16)
        return carry

    lax.fori_loop(0, n, pick, 0)


def roll_lanes(x, shift):
    w = x.shape[1]
    shift %= w
    if shift == 0:
        return x
    return jnp.concatenate([x[:, w - shift :], x[:, : w - shift]], axis=1)


def reach_of(hot):
    size = hot.shape[0]
    row = lax.broadcasted_iota(jnp.int32, (size, size), 0)
    col = lax.broadcasted_iota(jnp.int32, (size, size), 1)
    reach = hot + (row == col).astype(F32)
    for _ in range(size.bit_length()):
        twice = jnp.dot(reach.astype(BF16), reach.astype(BF16), preferred_element_type=F32)
        reach = jnp.minimum(twice, 1.0)
    return reach


def attend_kernel(
    pb, parents_ref, counts_ref, leaf_ref, table_ref, len_ref, q_ref, kv_ref, resid_ref, far_ref,
    cache_ref, w_out_ref, proj_ref, accepted_ref, pages, w_out, query, acc, peak, total, sem, w_sem,
):
    size = parents_ref.shape[1]
    qw, kw, half = q_ref.shape[1], kv_ref.shape[1], resid_ref.shape[1] // 2
    width = kw // 2
    heads = width // HEAD_DIM
    tail = qw + kw + half
    page_len = cache_ref.shape[2]
    keys = pb * page_len
    c = lax.axis_index("mlp")
    blocks = [(len_ref[s] + keys - 1) // keys for s in range(2)]

    for s in range(2):

        def fetch(b, carry):
            for i in range(pb):
                pltpu.make_async_copy(
                    cache_ref.at[table_ref[s, b * pb + i]], pages.at[s, b, i], sem.at[s, b]
                ).start()
            return carry

        lax.fori_loop(0, blocks[s], fetch, 0)
    w_copy = pltpu.make_async_copy(w_out_ref, w_out, w_sem)
    w_copy.start()

    row = lax.broadcasted_iota(jnp.int32, (size, size), 0)
    col = lax.broadcasted_iota(jnp.int32, (size, size), 1)
    lane = lax.broadcasted_iota(jnp.int32, (size, width), 1)
    tags = far_ref[:, tail:].astype(F32)
    near = [parent_matrix(parents_ref, s)[:, :size] for s in range(2)]
    far_hot = tags[:, :size]
    far_count = tags[:, COUNT_LANE : COUNT_LANE + 1]
    own_reach = [reach_of(hot) for hot in near]
    far_reach = reach_of(far_hot)

    before = (row < col).astype(BF16)
    for s in range(2):
        path = jnp.sum(jnp.where(row == leaf_ref[s], own_reach[s], 0.0), axis=0, keepdims=True)
        wide = jnp.broadcast_to(path, (size, size))
        ranks = jnp.dot(wide.astype(BF16), before, preferred_element_type=F32)
        select = jnp.where(ranks == row.astype(F32), wide, 0.0).astype(BF16)
        accepted_ref[s * size : (s + 1) * size, :] = jnp.dot(
            select, kv_ref[s * size : (s + 1) * size, :], preferred_element_type=F32
        ).astype(BF16)

    live = [
        jnp.where(col < counts_ref[0], own_reach[0], 0.0),
        jnp.where(col.astype(F32) < far_count, far_reach, 0.0),
    ]
    copies = GROUP * heads
    dims = (((1,), (1,)), ((), ()))
    for s in range(2):
        q_rows = (q_ref[:size, :] if s == 0 else far_ref[:, :qw]).astype(F32) * HEAD_DIM**-0.5
        parts = []
        for g in range(GROUP):
            for h in range(heads):
                piece = roll_lanes(q_rows[:, h * width : (h + 1) * width], (h - g) * HEAD_DIM)
                inside = (lane >= h * HEAD_DIM) & (lane < (h + 1) * HEAD_DIM)
                parts.append(jnp.where(inside, piece, 0.0))
        query[s] = jnp.concatenate(parts, axis=0).astype(BF16)
        draft = kv_ref[:size, :] if s == 0 else far_ref[:, qw : qw + kw]
        scores = lax.dot_general(query[s], draft[:, :width], dims, preferred_element_type=F32)
        open_ = jnp.concatenate([live[s]] * copies, axis=0) > 0.5
        scores = jnp.where(open_, scores, -1e30)
        top = jnp.max(scores, axis=1, keepdims=True)
        weights = jnp.where(open_, jnp.exp(scores - top), 0.0)
        peak[s] = jnp.broadcast_to(top, peak.shape[1:])
        total[s] = jnp.broadcast_to(jnp.sum(weights, axis=1, keepdims=True), total.shape[1:])
        acc[s] = jnp.dot(weights.astype(BF16), draft[:, width:], preferred_element_type=F32)

    for s in range(2):

        def step(b, carry):
            pltpu.make_async_copy(cache_ref.at[pl.ds(0, pb)], pages.at[s, b], sem.at[s, b]).wait()
            k = pages[s, b, :, 0].reshape(keys, width)
            v = pages[s, b, :, 1].reshape(keys, width)
            scores = lax.dot_general(query[s], k, dims, preferred_element_type=F32)
            places = b * keys + lax.broadcasted_iota(jnp.int32, scores.shape, 1)
            scores = jnp.where(places < len_ref[s], scores, -1e30)
            old = peak[s][:, :1]
            new = jnp.maximum(old, jnp.max(scores, axis=1, keepdims=True))
            weights = jnp.exp(scores - new)
            factor = jnp.exp(old - new)
            peak[s] = jnp.broadcast_to(new, peak.shape[1:])
            total[s] = total[s] * factor + jnp.sum(weights, axis=1, keepdims=True)
            acc[s] = acc[s] * factor + jnp.dot(weights.astype(BF16), v, preferred_element_type=F32)
            return carry

        lax.fori_loop(0, blocks[s], step, 0)

    done = []
    for s in range(2):
        result = acc[s] / total[s][:, :1]
        cols = []
        for h in range(heads):
            col_sum = jnp.zeros((size, width), F32)
            for g in range(GROUP):
                at = (g * heads + h) * size
                inside = (lane >= h * HEAD_DIM) & (lane < (h + 1) * HEAD_DIM)
                piece = jnp.where(inside, result[at : at + size], 0.0)
                col_sum = col_sum + roll_lanes(piece, (g - h) * HEAD_DIM)
            cols.append(col_sum)
        done.append(jnp.concatenate(cols, axis=1))
    attended = jnp.concatenate(done, axis=0).astype(BF16)
    w_copy.wait()
    proj_ref[...] = jnp.dot(attended, w_out[...], preferred_element_type=F32)
    mine = pl.ds(pl.multiple_of(c * half, 128), half)
    proj_ref[:size, mine] += resid_ref[:size, mine].astype(F32)
    proj_ref[size:, mine] += far_ref[:, qw + kw : tail].astype(F32)


def rms(values, gain):
    factor = lax.rsqrt(jnp.mean(values * values, axis=-1, keepdims=True) + EPS)
    return (values * factor * gain.astype(F32)).astype(BF16)


def layer_kernel(
    n, owners_ref, proj_ref, gain_mid_ref, gain_next_ref, w_in_hbm, w_down_hbm, w_next_hbm,
    hidden_ref, qkv_ref,
    w_in, w_down, w_next, other, mixed, rows_all, part, pair, ready, plane_in, line_out, line_in, final,
    w_sem, swap_sem, send_sem, recv_sem, fwd_send, fwd_recv, pair_send, pair_recv, rs_send, rs_recv,
):
    depth, plane = layout(n)
    me, z, p, c = position(n)
    size = ready.shape[1]
    width = ready.shape[2]
    loads = [
        pltpu.make_async_copy(src, dst, w_sem.at[i])
        for i, (src, dst) in enumerate(((w_in_hbm, w_in), (w_down_hbm, w_down), (w_next_hbm, w_next)))
    ]
    for load in loads:
        load.start()
    greet(n, True)
    partner = (me, 1 - c)
    swap = pltpu.make_async_remote_copy(
        proj_ref, other, swap_sem.at[0], swap_sem.at[1], device_id=partner, device_id_type=MESH
    )
    swap.start()
    swap.wait()
    both = (proj_ref[...] + other[...]).astype(BF16)
    mixed[0] = both[:size]
    mixed[1] = both[size:]
    mine = rows_all.at[c]
    rows_all[c, me] = rms(mixed[c].astype(F32), gain_mid_ref[...])

    line = line_copies(n, mine, send_sem, recv_sem)
    for copy in line:
        copy.start()
    by_back = []
    for back in range(depth):
        if back:
            line[back - 1].wait_recv()
        made = plane_copies(n, mine, back, send_sem, recv_sem)
        for copy in made:
            copy.start()
        by_back.append(made)
    loads[0].wait()
    loads[1].wait()

    def forward(back):
        group = pl.ds(lax.rem(z - back + depth, depth) * plane, plane)
        return pltpu.make_async_remote_copy(
            rows_all.at[c, group], rows_all.at[c, group],
            fwd_send.at[back], fwd_recv.at[back], device_id=partner, device_id_type=MESH,
        )

    def give(back):
        group = pl.ds(lax.rem(z - back + depth, depth) * plane, plane)
        return pltpu.make_async_remote_copy(
            part.at[1 - c, group], pair.at[group],
            pair_send.at[back], pair_recv.at[back], device_id=partner, device_id_type=MESH,
        )

    dims = (((1,), (1,)), ((), ()))
    for back in range(depth):
        for copy in by_back[back]:
            copy.wait_recv()
        forward(back).start()

    def feed(back, carry):
        forward(back).wait_recv()
        group = pl.ds(lax.rem(z - back + depth, depth) * plane, plane)
        x = rows_all[:, group].reshape(2 * plane * size, width)
        gate = lax.dot_general(x, w_in[0], dims, preferred_element_type=F32)
        up = lax.dot_general(x, w_in[1], dims, preferred_element_type=F32)
        hidden = (gate / (1.0 + jnp.exp(-gate)) * up).astype(BF16)
        y = jnp.dot(hidden, w_down[...], preferred_element_type=F32)
        part[:, group] = y.astype(BF16).reshape(2, plane, size, width)
        give(back).start()
        return carry

    lax.fori_loop(0, depth, feed, 0)
    part[c, me] = (part[c, me].astype(F32) + mixed[c].astype(F32)).astype(BF16)
    for back in range(depth):
        give(back).wait_recv()

    def gather_row(e, carry):
        d = e + c * (owners_ref[e] - e)
        ready[e] = (part[c, d].astype(F32) + pair[d].astype(F32)).astype(BF16)
        return carry

    lax.fori_loop(0, n, gather_row, 0)

    def to_plane(k, back):
        q = lax.rem(p + k, plane)
        i = (k - 1) * depth + back
        return pltpu.make_async_remote_copy(
            ready.at[lax.rem(z - back + depth, depth) * plane + q],
            plane_in.at[i],
            rs_send.at[i], rs_recv.at[i],
            device_id=(z * plane + q, c), device_id_type=MESH,
        )

    def to_line(back):
        i = (plane - 1) * depth + back
        return pltpu.make_async_remote_copy(
            line_out.at[back], line_in.at[back], rs_send.at[i], rs_recv.at[i],
            device_id=(lax.rem(z - back + depth, depth) * plane + p, c), device_id_type=MESH,
        )

    order = list(range(1, depth)) + [0]
    for back in order:
        for k in range(1, plane):
            to_plane(k, back).start()
    for back in order:
        for k in range(1, plane):
            to_plane(k, back).wait_recv()
        value = ready[lax.rem(z - back + depth, depth) * plane + p].astype(F32)
        for k in range(1, plane):
            value = value + plane_in[(k - 1) * depth + back].astype(F32)
        if back:
            line_out[back] = value.astype(BF16)
            to_line(back).start()
    for back in range(1, depth):
        to_line(back).wait_recv()
        value = value + line_in[back].astype(F32)
    final[c] = value.astype(BF16)
    last = pltpu.make_async_remote_copy(
        final.at[c], final.at[c], swap_sem.at[2], swap_sem.at[3], device_id=partner, device_id_type=MESH
    )
    last.start()
    loads[2].wait()
    last.wait()
    rows = jnp.concatenate([final[0], final[1]], axis=0)
    hidden_ref[...] = rows
    qkv_ref[...] = jnp.dot(
        rms(rows.astype(F32), gain_next_ref[...]), w_next[...], preferred_element_type=F32
    ).astype(BF16)
    for copy in line:
        copy.wait_send()
    for back in range(depth):
        for copy in by_back[back]:
            copy.wait_send()
        forward(back).wait_send()
        give(back).wait_send()
        for k in range(1, plane):
            to_plane(k, back).wait_send()
        if back:
            to_line(back).wait_send()


def per_device(
    n, resid, q_in, kv_in, parents, counts, accept_leaf, cache, held_table, held_len, prev_owner,
    w_out, gain_mid, w_in, w_down, gain_next, w_next,
):
    depth, plane = layout(n)
    size = parents.shape[1]
    width = resid.shape[1]
    qw = q_in.shape[1]
    kw = 2 * kv_in.shape[2]
    kv = kv_in.reshape(2 * size, kw)
    block = qw + kw + width // 2 + 128
    smem = pl.BlockSpec(memory_space=pltpu.SMEM)
    vmem = pl.BlockSpec(memory_space=VMEM)
    hbm = pl.BlockSpec(memory_space=pl.ANY)
    dma = pltpu.SemaphoreType.DMA
    sends = depth - 1 + depth * (plane - 1)
    far, owners = pl.pallas_call(
        functools.partial(share_kernel, n),
        out_shape=(
            jax.ShapeDtypeStruct((size, block), BF16),
            jax.ShapeDtypeStruct((n, 8, 128), jnp.int32),
        ),
        in_specs=[smem] * 3 + [vmem] * 3,
        out_specs=(vmem, vmem),
        scratch_shapes=[VMEM((n, size, block), BF16), dma((sends,)), dma((sends,))],
        compiler_params=pltpu.CompilerParams(
            collective_id=0, has_side_effects=True, vmem_limit_bytes=24 << 20
        ),
        name="share",
    )(parents, counts, prev_owner, q_in, kv, resid)

    pb = 4
    num_blocks = held_table.shape[1] // pb
    query_rows = size * qw // HEAD_DIM
    proj, accepted = pl.pallas_call(
        functools.partial(attend_kernel, pb),
        out_shape=(
            jax.ShapeDtypeStruct((2 * size, width), F32),
            jax.ShapeDtypeStruct((2 * size, kw), BF16),
        ),
        in_specs=[smem] * 5 + [vmem] * 4 + [hbm] * 2,
        out_specs=(vmem, vmem),
        scratch_shapes=[
            VMEM((2, num_blocks, pb) + cache.shape[1:], BF16),
            VMEM(w_out.shape, BF16),
            VMEM((2, query_rows, kw // 2), BF16),
            VMEM((2, query_rows, kw // 2), F32),
            VMEM((2, query_rows, 128), F32),
            VMEM((2, query_rows, 128), F32),
            dma((2, num_blocks)),
            dma,
        ],
        compiler_params=pltpu.CompilerParams(vmem_limit_bytes=48 << 20),
        name="attend",
    )(parents, counts, accept_leaf, held_table, held_len, q_in, kv, resid, far, cache, w_out)

    rows = (size, width)
    hidden_out, next_qkv = pl.pallas_call(
        functools.partial(layer_kernel, n),
        out_shape=(
            jax.ShapeDtypeStruct((2 * size, width), BF16),
            jax.ShapeDtypeStruct((2 * size, w_next.shape[1]), BF16),
        ),
        in_specs=[smem] + [vmem] * 3 + [hbm] * 3,
        out_specs=(vmem, vmem),
        scratch_shapes=[
            VMEM(w_in.shape, BF16),
            VMEM(w_down.shape, BF16),
            VMEM(w_next.shape, BF16),
            VMEM((2 * size, width), F32),
            VMEM((2,) + rows, BF16),
            VMEM((2, n) + rows, BF16),
            VMEM((2, n) + rows, BF16),
            VMEM((n,) + rows, BF16),
            VMEM((n,) + rows, BF16),
            VMEM(((plane - 1) * depth,) + rows, BF16),
            VMEM((depth,) + rows, BF16),
            VMEM((depth,) + rows, BF16),
            VMEM((2,) + rows, BF16),
            dma((3,)),
            dma((4,)),
            dma((sends,)),
            dma((sends,)),
            dma((depth,)),
            dma((depth,)),
            dma((depth,)),
            dma((depth,)),
            dma((plane * depth,)),
            dma((plane * depth,)),
        ],
        compiler_params=pltpu.CompilerParams(
            collective_id=1, has_side_effects=True, vmem_limit_bytes=60 << 20
        ),
        name="layer",
    )(
        owners[:, 0, 0], proj, gain_mid.reshape(1, width), gain_next.reshape(1, width),
        w_in, w_down, w_next,
    )
    return hidden_out, next_qkv, accepted.reshape(kv_in.shape)


def solution(mesh):
    placed = (
        P("req", None),
        P("req", "mlp"),
        P("req", None, "mlp"),
        P("req", None),
        P("req"),
        P("req"),
        P("req", None, None, "mlp"),
        P("req", None),
        P("req"),
        P("req"),
        P("mlp", None),
        P(),
        P(None, ("req", "mlp"), None),
        P(("req", "mlp"), None),
        P(),
        P(None, "mlp"),
    )
    return jax.shard_map(
        functools.partial(per_device, mesh.shape["req"]),
        mesh=mesh,
        in_specs=placed,
        out_specs=(P("req", None), P("req", "mlp"), P("req", None, "mlp")),
        check_vma=False,
    )
```

time: 558 us -> 102 us (0.18)
  waiting for transfers between devices: 217 us -> 0 us
  blocking collectives: 171 us -> 0 us
  Pallas kernels: 0 us -> 81.7 us
  local copies, waits for them, and re-layouts: 87 us -> 19 us
  matrix products: 51.2 us -> 0 us
  other arithmetic: 14.3 us -> 0 us
  between operations: 15.4 us -> 1.32 us
    all_gather x5 -> x0, blocking collectives: 154 us -> none  [the longest x1 40.2 us: per_device(): every_query = lax.all_gather(q_in[tree_len:], 'req', axis=0, tiled=True)]
    reduce_scatter x1 -> x0, waiting for transfers between devices: 138 us -> none  [per_device(): lax.psum_scatter(swiglu_rows(every_row, w_in, w_down), ('req', 'mlp'), sc...]
    pallas_call x0 -> x3, Pallas kernels: none -> 81.7 us  [the longest x1 51.8 us: per_device(): pl.pallas_call(functools.partial(layer_kernel, n), out_shape=(jax.ShapeDt...]
    all_gather x1 -> x0, waiting for transfers between devices: 63.7 us -> none  [per_device(): every_row = lax.all_gather(normed, 'req', axis=0, tiled=True)]
    dot_general x25 -> x0, matrix products: 51.2 us -> none  [the longest x6 21 us: attend_block(): jnp.einsum('sghqk,skge->sghqe', weights, value_rows.astype(jnp.float32),...]
    while x30 -> x0, local copies, waits for them, and re-layouts: 25.1 us -> none
    gather x6 -> x0, local copies, waits for them, and re-layouts: 24.4 us -> none  [attend_block(): gathered = cache[page_ids]]
    squeeze x12 -> x0, local copies, waits for them, and re-layouts: 21.6 us -> none  [the longest x6 13.9 us: attend_block(): value_rows = gathered[:, :, 1].reshape(2, block_keys, kv_local, HEAD_DIM)]
  transfers between devices with their start and end apart: 3 -> 0, of which waited for: 3 -> 0; matrix products, arithmetic and copies ran while one was open for 0% -> 0% of each run, Pallas kernels for 0% -> 0%
where the time goes in v1:
time: 102 us
  Pallas kernels  81.7 us (80%)
  local copies, waits for them, and re-layouts  19 us (19%)
  between operations  1.32 us (1%)
    pallas_call x1, Pallas kernels, per_device(): pl.pallas_call(functools.partial(layer_kernel, n), out_shape=(jax.ShapeDt...  51.8 us
    pallas_call x1, Pallas kernels, per_device(): pl.pallas_call(functools.partial(share_kernel, n), out_shape=(jax.ShapeDt...  24.3 us
    unnamed x29, local copies, waits for them, and re-layouts  14.9 us
    pallas_call x1, Pallas kernels, per_device(): pl.pallas_call(functools.partial(attend_kernel, pb), out_shape=(jax.Shape...  5.6 us

profile of v1, /device:TPU:0, one launch (start us, length us, event | category | flops | bytes accessed | tf_op | source)
XLA Modules:
  0.0 102.0 jit_solution(6605266922721683286)
XLA Ops:
  1.3 1.3 %reshape.19.gain_mid_ref = bf16[1,2048]{1,0:T(2,128)(2,1)} reshape(bf16[2048]{0:T(1024)(128)(2,1)} %param.27) | data formatting | bytes 8192 | tf_op jit(solution)/shard_map/reshape | solution.py:516
  2.6 1.3 %reshape.20.gain_next_ref = bf16[1,2048]{1,0:T(2,128)(2,1)} reshape(bf16[2048]{0:T(1024)(128)(2,1)} %param.30) | data formatting | bytes 8192 | tf_op jit(solution)/shard_map/reshape | solution.py:516
  3.9 0.8 copy.19
  4.6 0.0 copy-start.1
  4.6 0.9 copy-done.1
  5.5 0.0 copy-start.3
  5.5 0.8 copy-done.3
  6.4 0.0 copy-start.6
  6.4 0.7 copy-done.6
  7.0 0.0 copy-start.8
  7.0 0.7 copy-done.8
  7.7 24.3 %share.1 = (bf16[16,2688]{1,0:T(8,128)(2,1)S(1)}, s32[16,8,128]{2,1,0:T(8,128)S(1)}) custom-call(s32[2,16]{1,0:T(2,128)S(1)} %copy-done.6, s32[2]{0:T(128)S(1)} %copy-done.8, s32[1]{0:T(128)S(6)} %copy.22.owner_ref, bf16[32,1024]{1,0:T(8,128)(2,1)S(1)} %copy-done.3, bf16[32,512]{1,0:T(8,128)(2,1)S(1)} %bitcast.2, bf16[32,2048]{1,0:T(8,128)(2,1)S(1)} %copy-done.1), custom_call_target="tpu_custom_call" | custom-call | tf_op jit(solution)/shard_map/share/pallas_call | solution.py:437
  32.0 0.9 slice_reduce_fusion.owners_ref
  32.9 0.0 copy-start
  32.9 2.2 %copy-done = bf16[1024,2048]{1,0:T(8,128)(2,1)S(1)} copy-done((bf16[1024,2048]{1,0:T(8,128)(2,1)S(1)}, bf16[1024,2048]{1,0:T(8,128)(2,1)}, u32[]{:S(2)}) %copy-start) | copy-done | bytes 4194328
  35.1 0.0 copy-start.2
  35.1 0.9 copy-done.2
  36.0 0.0 copy-start.4
  36.0 0.8 copy-done.4
  36.8 0.0 copy-start.7
  36.8 0.7 copy-done.7
  37.5 0.0 copy-start.9
  37.5 0.7 copy-done.9
  38.1 0.0 copy-start.10
  38.1 0.7 copy-done.10
  38.8 0.0 copy-start.11
  38.8 0.7 copy-done.11
  39.5 0.0 copy-start.12
  39.5 0.7 copy-done.12
  40.1 5.6 %attend.1 = (f32[32,2048]{1,0:T(8,128)S(1)}, bf16[32,512]{1,0:T(8,128)(2,1)S(1)}) custom-call(s32[2,16]{1,0:T(2,128)S(1)} %copy-done.7, s32[2]{0:T(128)S(1)} %copy-done.9, s32[2]{0:T(128)S(1)} %copy-done.11, s32[2,48]{1,0:T(2,128)S(1)} %copy-done.10, s32[2]{0:T(128)S(1)} %copy-done.12, bf16[32,1024]{1,0:T(8,128)(2,1)S(1)} %copy-done.4, ...), custom_call_target="tpu_custom_call" | custom-call | tf_op jit(solution)/shard_map/attend/pallas_call | solution.py:455
  45.7 0.0 copy-start.5
  45.7 0.7 copy-done.5
  46.4 51.8 %layer.1 = (bf16[32,2048]{1,0:T(8,128)(2,1)}, bf16[32,1536]{1,0:T(8,128)(2,1)}) custom-call(s32[16]{0:T(128)} %slice_reduce_fusion.owners_ref, f32[32,2048]{1,0:T(8,128)} %copy-done.5, bf16[1,2048]{1,0:T(2,128)(2,1)} %reshape.19.gain_mid_ref, bf16[1,2048]{1,0:T(2,128)(2,1)} %reshape.20.gain_next_ref, bf16[2,256,2048]{2,1,0:T(8,128)(2,1)} %w_in_hbm.1, ...), custom_call_target="tpu_custom_call" | custom-call | tf_op jit(solution)/shard_map/layer/pallas_call | solution.py:478
  98.3 0.6 reshape.21
  98.9 1.6 %copy.23 = bf16[32,2048]{1,0:T(8,128)(2,1)} copy(bf16[32,2048]{1,0:T(8,128)(2,1)} %get-tuple-element.18) | data formatting | bytes 262144
  100.5 1.5 %copy.24 = bf16[32,1536]{1,0:T(8,128)(2,1)} copy(bf16[32,1536]{1,0:T(8,128)(2,1)} %get-tuple-element.19) | data formatting | bytes 196608
Async XLA Ops:
  4.6 0.9 copy-start.1
  5.5 0.8 copy-start.3
  6.4 0.7 copy-start.6
  7.0 0.7 copy-start.8
  32.9 2.2 %copy-start = (bf16[1024,2048]{1,0:T(8,128)(2,1)S(1)}, bf16[1024,2048]{1,0:T(8,128)(2,1)}, u32[]{:S(2)}) copy-start(bf16[1024,2048]{1,0:T(8,128)(2,1)} %w_out_ref.1) | copy-start | bytes 12582916
  35.1 0.9 copy-start.2
  36.0 0.8 copy-start.4
  36.8 0.7 copy-start.7
  37.5 0.7 copy-start.9
  38.1 0.7 copy-start.10
  38.8 0.7 copy-start.11
  39.5 0.7 copy-start.12
  45.7 0.7 copy-start.5

commit v2 on v1

--- a/solution.py
+++ b/solution.py
@@ -63,20 +63,36 @@
 def plane_copies(n, ref, back, send_sem, recv_sem):
     depth, plane = layout(n)
     me, z, p, c = position(n)
-    block = lax.rem(z - back + depth, depth) * plane + p
-    made = []
-    for k in range(1, plane):
-        made.append(
-            pltpu.make_async_remote_copy(
-                ref.at[block],
-                ref.at[block],
-                send_sem.at[depth - 1 + back * (plane - 1) + k - 1],
-                recv_sem.at[depth - 1 + back * (plane - 1) + k - 1],
-                device_id=(z * plane + lax.rem(p + k, plane), c),
-                device_id_type=MESH,
-            )
+    base = lax.rem(z - back + depth, depth) * plane
+
+    def copy(view, place, i):
+        at = depth - 1 + back * plane + i
+        return pltpu.make_async_remote_copy(
+            view, view, send_sem.at[at], recv_sem.at[at],
+            device_id=(z * plane + place, c), device_id_type=MESH,
         )
-    return made
+
+    if plane != 4:
+        return [copy(ref.at[base + p], lax.rem(p + k, plane), k - 1) for k in range(1, plane)], []
+    width = ref.shape[-1]
+    cut = width // 256 * 128
+    side, across = p + 1 - 2 * lax.rem(p, 2), lax.rem(p + 2, 4)
+    first = [copy(ref.at[base + p], side, 0), copy(ref.at[base + p], across, 1)]
+    relays = [
+        copy(ref.at[base + side, :, pl.ds(0, cut)], across, 2),
+        copy(ref.at[base + across, :, pl.ds(cut, width - cut)], side, 3),
+    ]
+    return first, relays
+
+
+def run_plane(made, started):
+    first, relays = made
+    for i, relay in enumerate(relays):
+        first[i].wait_recv()
+        relay.start()
+    started += first + relays
+    for copy in relays if relays else first:
+        copy.wait_recv()
 
 
 def parent_matrix(parents_ref, r):
@@ -89,9 +105,16 @@
     return hot
 
 
+def fetch_all(sem, *pairs):
+    loads = [pltpu.make_async_copy(src, dst, sem.at[i]) for i, (src, dst) in enumerate(pairs)]
+    for load in loads:
+        load.start()
+    return loads
+
+
 def share_kernel(
     n, parents_ref, counts_ref, owner_ref, q_ref, kv_ref, resid_ref,
-    out_ref, owners_ref, blocks, send_sem, recv_sem,
+    out_ref, owners_ref, blocks, send_sem, recv_sem, parents_s, counts_s, owner_s, load_sem,
 ):
     depth, plane = layout(n)
     me, z, p, c = position(n)
@@ -99,27 +122,39 @@
     qw, kw, half = q_ref.shape[1], kv_ref.shape[1], resid_ref.shape[1] // 2
     tail = qw + kw + half
     lane = lax.broadcasted_iota(jnp.int32, (rows, 128), 1)
-    info = parent_matrix(parents_ref, 1)
-    info = jnp.where(lane == COUNT_LANE, counts_ref[1].astype(F32), info)
-    info = jnp.where(lane == OWNER_LANE, owner_ref[0].astype(F32), info)
-    blocks[me, :, :qw] = q_ref[rows:, :]
-    blocks[me, :, qw : qw + kw] = kv_ref[rows:, :]
-    blocks[me, :, qw + kw : tail] = resid_ref[rows:, pl.ds(pl.multiple_of(c * half, 128), half)]
+    second = pl.ds(rows, rows)
+    own_half = pl.ds(pl.multiple_of(c * half, 128), half)
+    loads = fetch_all(
+        load_sem,
+        (parents_ref, parents_s),
+        (counts_ref, counts_s),
+        (owner_ref, owner_s),
+        (q_ref.at[second], blocks.at[me, :, pl.ds(0, qw)]),
+        (kv_ref.at[second], blocks.at[me, :, pl.ds(qw, kw)]),
+        (resid_ref.at[second, own_half], blocks.at[me, :, pl.ds(qw + kw, half)]),
+    )
+    greet(n, False)
+    for load in loads:
+        load.wait()
+    info = parent_matrix(parents_s, 1)
+    info = jnp.where(lane == COUNT_LANE, counts_s[1].astype(F32), info)
+    info = jnp.where(lane == OWNER_LANE, owner_s[0].astype(F32), info)
     blocks[me, :, tail:] = info.astype(BF16)
-    greet(n, False)
     line = line_copies(n, blocks, send_sem, recv_sem)
     for copy in line:
         copy.start()
     started = list(line)
+    waiting = None
     for back in range(depth):
         if back:
             line[back - 1].wait_recv()
         made = plane_copies(n, blocks, back, send_sem, recv_sem)
-        for copy in made:
+        for copy in made[0]:
             copy.start()
-        started += made
-    for copy in started[depth - 1 :]:
-        copy.wait_recv()
+        if waiting:
+            run_plane(waiting, started)
+        waiting = made
+    run_plane(waiting, started)
     for copy in started:
         copy.wait_send()
 
@@ -128,7 +163,7 @@
     def pick(j, carry):
         tags = blocks[j, :, tail:].astype(F32)
         owner = jnp.sum(jnp.where(lane == OWNER_LANE, tags, 0.0), axis=1, keepdims=True)
-        owners_ref[j] = jnp.broadcast_to(owner, (rows, 128))[:8].astype(jnp.int32)
+        owners_ref[pl.ds(j, 1), :] = jnp.broadcast_to(owner, (rows, 128))[:1].astype(jnp.int32)
         mine = (owner == me.astype(F32)).astype(F32)
         out_ref[...] = (out_ref[...].astype(F32) + blocks[j].astype(F32) * mine).astype(BF16)
         return carry
@@ -158,7 +193,17 @@
 def attend_kernel(
     pb, parents_ref, counts_ref, leaf_ref, table_ref, len_ref, q_ref, kv_ref, resid_ref, far_ref,
     cache_ref, w_out_ref, proj_ref, accepted_ref, pages, w_out, query, acc, peak, total, sem, w_sem,
+    parents_s, counts_s, leaf_s, table_s, len_s, q_v, kv_v, resid_v, load_sem,
 ):
+    loads = fetch_all(
+        load_sem,
+        (table_ref, table_s), (len_ref, len_s), (parents_ref, parents_s), (counts_ref, counts_s),
+        (leaf_ref, leaf_s), (q_ref, q_v), (kv_ref, kv_v), (resid_ref, resid_v),
+    )
+    loads[0].wait()
+    loads[1].wait()
+    parents_ref, counts_ref, leaf_ref, table_ref, len_ref = parents_s, counts_s, leaf_s, table_s, len_s
+    q_ref, kv_ref, resid_ref = q_v, kv_v, resid_v
     size = parents_ref.shape[1]
     qw, kw, half = q_ref.shape[1], kv_ref.shape[1], resid_ref.shape[1] // 2
     width = kw // 2
@@ -181,6 +226,8 @@
         lax.fori_loop(0, blocks[s], fetch, 0)
     w_copy = pltpu.make_async_copy(w_out_ref, w_out, w_sem)
     w_copy.start()
+    for load in loads[2:]:
+        load.wait()
 
     row = lax.broadcasted_iota(jnp.int32, (size, size), 0)
     col = lax.broadcasted_iota(jnp.int32, (size, size), 1)
@@ -270,7 +317,7 @@
 
 def rms(values, gain):
     factor = lax.rsqrt(jnp.mean(values * values, axis=-1, keepdims=True) + EPS)
-    return (values * factor * gain.astype(F32)).astype(BF16)
+    return (values * factor * gain.astype(F32).reshape(1, -1)).astype(BF16)
 
 
 def layer_kernel(
@@ -305,17 +352,6 @@
     line = line_copies(n, mine, send_sem, recv_sem)
     for copy in line:
         copy.start()
-    by_back = []
-    for back in range(depth):
-        if back:
-            line[back - 1].wait_recv()
-        made = plane_copies(n, mine, back, send_sem, recv_sem)
-        for copy in made:
-            copy.start()
-        by_back.append(made)
-    loads[0].wait()
-    loads[1].wait()
-
     def forward(back):
         group = pl.ds(lax.rem(z - back + depth, depth) * plane, plane)
         return pltpu.make_async_remote_copy(
@@ -331,12 +367,8 @@
         )
 
     dims = (((1,), (1,)), ((), ()))
-    for back in range(depth):
-        for copy in by_back[back]:
-            copy.wait_recv()
-        forward(back).start()
-
-    def feed(back, carry):
+
+    def feed(back):
         forward(back).wait_recv()
         group = pl.ds(lax.rem(z - back + depth, depth) * plane, plane)
         x = rows_all[:, group].reshape(2 * plane * size, width)
@@ -346,15 +378,32 @@
         y = jnp.dot(hidden, w_down[...], preferred_element_type=F32)
         part[:, group] = y.astype(BF16).reshape(2, plane, size, width)
         give(back).start()
-        return carry
-
-    lax.fori_loop(0, depth, feed, 0)
+
+    started = list(line)
+    made = plane_copies(n, mine, 0, send_sem, recv_sem)
+    for copy in made[0]:
+        copy.start()
+    for back in range(depth):
+        waiting = made
+        if back + 1 < depth:
+            line[back].wait_recv()
+            made = plane_copies(n, mine, back + 1, send_sem, recv_sem)
+            for copy in made[0]:
+                copy.start()
+        run_plane(waiting, started)
+        forward(back).start()
+        if back == 0:
+            loads[0].wait()
+            loads[1].wait()
+        else:
+            feed(back - 1)
+    feed(depth - 1)
     part[c, me] = (part[c, me].astype(F32) + mixed[c].astype(F32)).astype(BF16)
     for back in range(depth):
         give(back).wait_recv()
 
     def gather_row(e, carry):
-        d = e + c * (owners_ref[e] - e)
+        d = e + c * (owners_ref[e, 0] - e)
         ready[e] = (part[c, d].astype(F32) + pair[d].astype(F32)).astype(BF16)
         return carry
 
@@ -405,11 +454,9 @@
     qkv_ref[...] = jnp.dot(
         rms(rows.astype(F32), gain_next_ref[...]), w_next[...], preferred_element_type=F32
     ).astype(BF16)
-    for copy in line:
+    for copy in started:
         copy.wait_send()
     for back in range(depth):
-        for copy in by_back[back]:
-            copy.wait_send()
         forward(back).wait_send()
         give(back).wait_send()
         for k in range(1, plane):
@@ -433,18 +480,25 @@
     vmem = pl.BlockSpec(memory_space=VMEM)
     hbm = pl.BlockSpec(memory_space=pl.ANY)
     dma = pltpu.SemaphoreType.DMA
-    sends = depth - 1 + depth * (plane - 1)
+
+    def smem_of(array):
+        return pltpu.SMEM(array.shape, array.dtype)
+
+    sends = depth - 1 + depth * plane
     far, owners = pl.pallas_call(
         functools.partial(share_kernel, n),
         out_shape=(
             jax.ShapeDtypeStruct((size, block), BF16),
-            jax.ShapeDtypeStruct((n, 8, 128), jnp.int32),
+            jax.ShapeDtypeStruct((n, 128), jnp.int32),
         ),
-        in_specs=[smem] * 3 + [vmem] * 3,
+        in_specs=[hbm] * 6,
         out_specs=(vmem, vmem),
-        scratch_shapes=[VMEM((n, size, block), BF16), dma((sends,)), dma((sends,))],
+        scratch_shapes=[
+            VMEM((n, size, block), BF16), dma((sends,)), dma((sends,)),
+            smem_of(parents), smem_of(counts), smem_of(prev_owner), dma((6,)),
+        ],
         compiler_params=pltpu.CompilerParams(
-            collective_id=0, has_side_effects=True, vmem_limit_bytes=24 << 20
+            collective_id=0, has_side_effects=True, vmem_limit_bytes=60 << 20
         ),
         name="share",
     )(parents, counts, prev_owner, q_in, kv, resid)
@@ -458,7 +512,7 @@
             jax.ShapeDtypeStruct((2 * size, width), F32),
             jax.ShapeDtypeStruct((2 * size, kw), BF16),
         ),
-        in_specs=[smem] * 5 + [vmem] * 4 + [hbm] * 2,
+        in_specs=[hbm] * 8 + [vmem] + [hbm] * 2,
         out_specs=(vmem, vmem),
         scratch_shapes=[
             VMEM((2, num_blocks, pb) + cache.shape[1:], BF16),
@@ -469,8 +523,10 @@
             VMEM((2, query_rows, 128), F32),
             dma((2, num_blocks)),
             dma,
+            smem_of(parents), smem_of(counts), smem_of(accept_leaf), smem_of(held_table), smem_of(held_len),
+            VMEM(q_in.shape, BF16), VMEM(kv.shape, BF16), VMEM(resid.shape, BF16), dma((8,)),
         ],
-        compiler_params=pltpu.CompilerParams(vmem_limit_bytes=48 << 20),
+        compiler_params=pltpu.CompilerParams(vmem_limit_bytes=60 << 20),
         name="attend",
     )(parents, counts, accept_leaf, held_table, held_len, q_in, kv, resid, far, cache, w_out)
 
@@ -513,7 +569,7 @@
         ),
         name="layer",
     )(
-        owners[:, 0, 0], proj, gain_mid.reshape(1, width), gain_next.reshape(1, width),
+        owners, proj, gain_mid, gain_next,
         w_in, w_down, w_next,
     )
     return hidden_out, next_qkv, accepted.reshape(kv_in.shape)

time: 102 us -> 99.4 us (0.975)
  local copies, waits for them, and re-layouts: 19 us -> 5.12 us
  Pallas kernels: 81.7 us -> 92.8 us
    unnamed x29 -> x5, local copies, waits for them, and re-layouts: 14.9 us -> 4.49 us
    pallas_call x1, Pallas kernels: 24.3 us -> 30.7 us  [per_device(): pl.pallas_call(functools.partial(share_kernel, n), out_shape=(jax.ShapeDt...]
    pallas_call x1, Pallas kernels: 51.8 us -> 54.9 us  [per_device(): pl.pallas_call(functools.partial(layer_kernel, n), out_shape=(jax.ShapeDt...]
    reshape x2 -> x0, local copies, waits for them, and re-layouts: 2.58 us -> none  [the longest x1 1.29 us: per_device(): gain_mid.reshape(1, width)]
    pallas_call x1, Pallas kernels: 5.6 us -> 7.3 us  [per_device(): pl.pallas_call(functools.partial(attend_kernel, pb), out_shape=(jax.Shape...]
where the time goes in v2:
time: 99.4 us; the launch traced here: 99.3 us
  Pallas kernels  92.8 us (93%)
  local copies, waits for them, and re-layouts  5.12 us (5%)
  between operations  1.32 us (1%)
    pallas_call x1, Pallas kernels, per_device(): pl.pallas_call(functools.partial(layer_kernel, n), out_shape=(jax.ShapeDt...  54.9 us
    pallas_call x1, Pallas kernels, per_device(): pl.pallas_call(functools.partial(share_kernel, n), out_shape=(jax.ShapeDt...  30.7 us
    pallas_call x1, Pallas kernels, per_device(): pl.pallas_call(functools.partial(attend_kernel, pb), out_shape=(jax.Shape...  7.3 us
    unnamed x5, local copies, waits for them, and re-layouts  4.49 us

profile of v2, /device:TPU:0, one launch (start us, length us, event | category | flops | bytes accessed | tf_op | source)
XLA Modules:
  0.0 99.3 jit_solution(17591348825664510481)
XLA Ops:
  1.3 1.4 %copy.19 = bf16[4,8,2,256]{3,1,2,0:T(8,128)(2,1)} copy(bf16[4,8,2,256]{3,2,1,0:T(2,128)(2,1)} %bitcast.4) | data formatting | bytes 65536
  2.7 30.7 %share.1 = (bf16[16,2688]{1,0:T(8,128)(2,1)}, s32[16,128]{1,0:T(8,128)}) custom-call(s32[2,16]{1,0:T(2,128)} %parents_ref.3, s32[2]{0:T(128)} %counts_ref.3, s32[1]{0:T(128)S(6)} %copy.22.owner_ref, bf16[32,1024]{1,0:T(8,128)(2,1)} %q_ref.3, bf16[32,512]{1,0:T(8,128)(2,1)} %bitcast.2, bf16[32,2048]{1,0:T(8,128)(2,1)} %resid_ref.3), custom_call_target="tpu_custom_call" | custom-call | tf_op jit(solution)/shard_map/share/pallas_call | solution.py:488
  33.3 7.3 %attend.1 = (f32[32,2048]{1,0:T(8,128)}, bf16[32,512]{1,0:T(8,128)(2,1)}) custom-call(s32[2,16]{1,0:T(2,128)} %parents_ref.3, s32[2]{0:T(128)} %counts_ref.3, s32[2]{0:T(128)} %leaf_ref.1, s32[2,48]{1,0:T(2,128)} %table_ref.1, s32[2]{0:T(128)} %len_ref.1, bf16[32,1024]{1,0:T(8,128)(2,1)} %q_ref.3, bf16[32,512]{1,0:T(8,128)(2,1)} %bitcast.3, ...), custom_call_target="tpu_custom_call" | custom-call | tf_op jit(solution)/shard_map/attend/pallas_call | solution.py:509
  40.6 0.0 copy-start
  40.6 54.9 %layer.1 = (bf16[32,2048]{1,0:T(8,128)(2,1)}, bf16[32,1536]{1,0:T(8,128)(2,1)}) custom-call(s32[16,128]{1,0:T(8,128)} %get-tuple-element.9.owners_ref, f32[32,2048]{1,0:T(8,128)} %get-tuple-element.11.proj_ref, bf16[2048]{0:T(1024)(128)(2,1)} %gain_mid_ref.1, bf16[2048]{0:T(1024)(128)(2,1)} %gain_next_ref.1, bf16[2,256,2048]{2,1,0:T(8,128)(2,1)} %w_in_hbm.1, ...), custom_call_target="tpu_custom_call" | custom-call | tf_op jit(solution)/shard_map/layer/pallas_call | solution.py:534
  95.5 0.0 copy-done
  95.5 0.6 reshape.13
  96.2 1.6 %copy.23 = bf16[32,2048]{1,0:T(8,128)(2,1)} copy(bf16[32,2048]{1,0:T(8,128)(2,1)} %get-tuple-element.18) | data formatting | bytes 262144
  97.7 1.5 %copy.24 = bf16[32,1536]{1,0:T(8,128)(2,1)} copy(bf16[32,1536]{1,0:T(8,128)(2,1)} %get-tuple-element.19) | data formatting | bytes 196608
Async XLA Ops:
  40.6 54.9 %copy-start = (bf16[32,512]{1,0:T(8,128)(2,1)S(1)}, bf16[32,512]{1,0:T(8,128)(2,1)}, u32[]{:S(2)}) copy-start(bf16[32,512]{1,0:T(8,128)(2,1)} %get-tuple-element.14) | copy-start | bytes 98308

commit v3 on v2

--- a/solution.py
+++ b/solution.py
@@ -72,17 +72,7 @@
             device_id=(z * plane + place, c), device_id_type=MESH,
         )
 
-    if plane != 4:
-        return [copy(ref.at[base + p], lax.rem(p + k, plane), k - 1) for k in range(1, plane)], []
-    width = ref.shape[-1]
-    cut = width // 256 * 128
-    side, across = p + 1 - 2 * lax.rem(p, 2), lax.rem(p + 2, 4)
-    first = [copy(ref.at[base + p], side, 0), copy(ref.at[base + p], across, 1)]
-    relays = [
-        copy(ref.at[base + side, :, pl.ds(0, cut)], across, 2),
-        copy(ref.at[base + across, :, pl.ds(cut, width - cut)], side, 3),
-    ]
-    return first, relays
+    return [copy(ref.at[base + p], lax.rem(p + k, plane), k - 1) for k in range(1, plane)], []
 
 
 def run_plane(made, started):

time: 99.4 us -> 90.1 us (0.906); the launches traced: 99.3 us -> 91.2 us
  Pallas kernels: 92.8 us -> 84.7 us
    pallas_call x1, Pallas kernels: 30.7 us -> 25.3 us  [per_device(): pl.pallas_call(functools.partial(share_kernel, n), out_shape=(jax.ShapeDt...]
    pallas_call x1, Pallas kernels: 54.9 us -> 52.1 us  [per_device(): pl.pallas_call(functools.partial(layer_kernel, n), out_shape=(jax.ShapeDt...]
where the time goes in v3:
time: 90.1 us; the launch traced here: 91.2 us
  Pallas kernels  84.7 us (94%)
  local copies, waits for them, and re-layouts  5.12 us (6%)
  between operations  1.32 us (1%)
    pallas_call x1, Pallas kernels, per_device(): pl.pallas_call(functools.partial(layer_kernel, n), out_shape=(jax.ShapeDt...  52.1 us
    pallas_call x1, Pallas kernels, per_device(): pl.pallas_call(functools.partial(share_kernel, n), out_shape=(jax.ShapeDt...  25.3 us
    pallas_call x1, Pallas kernels, per_device(): pl.pallas_call(functools.partial(attend_kernel, pb), out_shape=(jax.Shape...  7.3 us
    unnamed x5, local copies, waits for them, and re-layouts  4.49 us

profile of v3, /device:TPU:0, one launch (start us, length us, event | category | flops | bytes accessed | tf_op | source)
XLA Modules:
  0.0 91.2 jit_solution(4141760561926285976)
XLA Ops:
  1.3 1.4 %copy.19 = bf16[4,8,2,256]{3,1,2,0:T(8,128)(2,1)} copy(bf16[4,8,2,256]{3,2,1,0:T(2,128)(2,1)} %bitcast.4) | data formatting | bytes 65536
  2.7 25.3 %share.1 = (bf16[16,2688]{1,0:T(8,128)(2,1)}, s32[16,128]{1,0:T(8,128)}) custom-call(s32[2,16]{1,0:T(2,128)} %parents_ref.3, s32[2]{0:T(128)} %counts_ref.3, s32[1]{0:T(128)S(6)} %copy.22.owner_ref, bf16[32,1024]{1,0:T(8,128)(2,1)} %q_ref.3, bf16[32,512]{1,0:T(8,128)(2,1)} %bitcast.2, bf16[32,2048]{1,0:T(8,128)(2,1)} %resid_ref.3), custom_call_target="tpu_custom_call" | custom-call | tf_op jit(solution)/shard_map/share/pallas_call | solution.py:478
  28.0 7.3 %attend.1 = (f32[32,2048]{1,0:T(8,128)}, bf16[32,512]{1,0:T(8,128)(2,1)}) custom-call(s32[2,16]{1,0:T(2,128)} %parents_ref.3, s32[2]{0:T(128)} %counts_ref.3, s32[2]{0:T(128)} %leaf_ref.1, s32[2,48]{1,0:T(2,128)} %table_ref.1, s32[2]{0:T(128)} %len_ref.1, bf16[32,1024]{1,0:T(8,128)(2,1)} %q_ref.3, bf16[32,512]{1,0:T(8,128)(2,1)} %bitcast.3, ...), custom_call_target="tpu_custom_call" | custom-call | tf_op jit(solution)/shard_map/attend/pallas_call | solution.py:499
  35.3 0.0 copy-start
  35.3 52.1 %layer.1 = (bf16[32,2048]{1,0:T(8,128)(2,1)}, bf16[32,1536]{1,0:T(8,128)(2,1)}) custom-call(s32[16,128]{1,0:T(8,128)} %get-tuple-element.9.owners_ref, f32[32,2048]{1,0:T(8,128)} %get-tuple-element.11.proj_ref, bf16[2048]{0:T(1024)(128)(2,1)} %gain_mid_ref.1, bf16[2048]{0:T(1024)(128)(2,1)} %gain_next_ref.1, bf16[2,256,2048]{2,1,0:T(8,128)(2,1)} %w_in_hbm.1, ...), custom_call_target="tpu_custom_call" | custom-call | tf_op jit(solution)/shard_map/layer/pallas_call | solution.py:524
  87.4 0.0 copy-done
  87.4 0.6 reshape.13
  88.1 1.6 %copy.23 = bf16[32,2048]{1,0:T(8,128)(2,1)} copy(bf16[32,2048]{1,0:T(8,128)(2,1)} %get-tuple-element.18) | data formatting | bytes 262144
  89.6 1.5 %copy.24 = bf16[32,1536]{1,0:T(8,128)(2,1)} copy(bf16[32,1536]{1,0:T(8,128)(2,1)} %get-tuple-element.19) | data formatting | bytes 196608
Async XLA Ops:
  35.3 52.1 %copy-start = (bf16[32,512]{1,0:T(8,128)(2,1)S(1)}, bf16[32,512]{1,0:T(8,128)(2,1)}, u32[]{:S(2)}) copy-start(bf16[32,512]{1,0:T(8,128)(2,1)} %get-tuple-element.14) | copy-start | bytes 98308

commit v4 on v3

--- a/solution.py
+++ b/solution.py
@@ -1,4 +1,5 @@
 import functools
+import math
 
 import jax
 import jax.numpy as jnp
@@ -271,8 +272,8 @@
             k = pages[s, b, :, 0].reshape(keys, width)
             v = pages[s, b, :, 1].reshape(keys, width)
             scores = lax.dot_general(query[s], k, dims, preferred_element_type=F32)
-            places = b * keys + lax.broadcasted_iota(jnp.int32, scores.shape, 1)
-            scores = jnp.where(places < len_ref[s], scores, -1e30)
+            places = b * keys + lax.broadcasted_iota(jnp.int32, (1, keys), 1)
+            scores = scores + jnp.where(places < len_ref[s], 0.0, -1e30)
             old = peak[s][:, :1]
             new = jnp.maximum(old, jnp.max(scores, axis=1, keepdims=True))
             weights = jnp.exp(scores - new)
@@ -493,7 +494,7 @@
         name="share",
     )(parents, counts, prev_owner, q_in, kv, resid)
 
-    pb = 4
+    pb = math.gcd(held_table.shape[1], 8)
     num_blocks = held_table.shape[1] // pb
     query_rows = size * qw // HEAD_DIM
     proj, accepted = pl.pallas_call(

time: 90.1 us -> 86.6 us (0.961); the launches traced: 91.2 us -> 86 us
  Pallas kernels: 84.7 us -> 79.6 us
    pallas_call x1, Pallas kernels: 52.1 us -> 41.3 us  [per_device(): pl.pallas_call(functools.partial(layer_kernel, n), out_shape=(jax.ShapeDt...]
    pallas_call x1, Pallas kernels: 7.3 us -> 12.9 us  [per_device(): pl.pallas_call(functools.partial(attend_kernel, pb), out_shape=(jax.Shape...]
where the time goes in v4:
time: 86.6 us; the launch traced here: 86 us
  Pallas kernels  79.6 us (92%)
  local copies, waits for them, and re-layouts  5.12 us (6%)
  between operations  1.32 us (2%)
    pallas_call x1, Pallas kernels, per_device(): pl.pallas_call(functools.partial(layer_kernel, n), out_shape=(jax.ShapeDt...  41.3 us
    pallas_call x1, Pallas kernels, per_device(): pl.pallas_call(functools.partial(share_kernel, n), out_shape=(jax.ShapeDt...  25.3 us
    pallas_call x1, Pallas kernels, per_device(): pl.pallas_call(functools.partial(attend_kernel, pb), out_shape=(jax.Shape...  12.9 us
    unnamed x5, local copies, waits for them, and re-layouts  4.49 us

profile of v4, /device:TPU:0, one launch (start us, length us, event | category | flops | bytes accessed | tf_op | source)
XLA Modules:
  0.0 86.0 jit_solution(7790366960578857554)
XLA Ops:
  1.3 1.4 %copy.19 = bf16[4,8,2,256]{3,1,2,0:T(8,128)(2,1)} copy(bf16[4,8,2,256]{3,2,1,0:T(2,128)(2,1)} %bitcast.4) | data formatting | bytes 65536
  2.7 25.3 %share.1 = (bf16[16,2688]{1,0:T(8,128)(2,1)}, s32[16,128]{1,0:T(8,128)}) custom-call(s32[2,16]{1,0:T(2,128)} %parents_ref.3, s32[2]{0:T(128)} %counts_ref.3, s32[1]{0:T(128)S(6)} %copy.22.owner_ref, bf16[32,1024]{1,0:T(8,128)(2,1)} %q_ref.3, bf16[32,512]{1,0:T(8,128)(2,1)} %bitcast.2, bf16[32,2048]{1,0:T(8,128)(2,1)} %resid_ref.3), custom_call_target="tpu_custom_call" | custom-call | tf_op jit(solution)/shard_map/share/pallas_call | solution.py:479
  28.0 12.9 %attend.1 = (f32[32,2048]{1,0:T(8,128)}, bf16[32,512]{1,0:T(8,128)(2,1)}) custom-call(s32[2,16]{1,0:T(2,128)} %parents_ref.3, s32[2]{0:T(128)} %counts_ref.3, s32[2]{0:T(128)} %leaf_ref.1, s32[2,48]{1,0:T(2,128)} %table_ref.1, s32[2]{0:T(128)} %len_ref.1, bf16[32,1024]{1,0:T(8,128)(2,1)} %q_ref.3, bf16[32,512]{1,0:T(8,128)(2,1)} %bitcast.3, ...), custom_call_target="tpu_custom_call" | custom-call | tf_op jit(solution)/shard_map/attend/pallas_call | solution.py:500
  40.9 0.0 copy-start
  40.9 41.3 %layer.1 = (bf16[32,2048]{1,0:T(8,128)(2,1)}, bf16[32,1536]{1,0:T(8,128)(2,1)}) custom-call(s32[16,128]{1,0:T(8,128)} %get-tuple-element.9.owners_ref, f32[32,2048]{1,0:T(8,128)} %get-tuple-element.11.proj_ref, bf16[2048]{0:T(1024)(128)(2,1)} %gain_mid_ref.1, bf16[2048]{0:T(1024)(128)(2,1)} %gain_next_ref.1, bf16[2,256,2048]{2,1,0:T(8,128)(2,1)} %w_in_hbm.1, ...), custom_call_target="tpu_custom_call" | custom-call | tf_op jit(solution)/shard_map/layer/pallas_call | solution.py:525
  82.2 0.0 copy-done
  82.3 0.6 reshape.13
  82.9 1.6 %copy.23 = bf16[32,2048]{1,0:T(8,128)(2,1)} copy(bf16[32,2048]{1,0:T(8,128)(2,1)} %get-tuple-element.18) | data formatting | bytes 262144
  84.5 1.5 %copy.24 = bf16[32,1536]{1,0:T(8,128)(2,1)} copy(bf16[32,1536]{1,0:T(8,128)(2,1)} %get-tuple-element.19) | data formatting | bytes 196608
Async XLA Ops:
  40.9 41.3 %copy-start = (bf16[32,512]{1,0:T(8,128)(2,1)S(1)}, bf16[32,512]{1,0:T(8,128)(2,1)}, u32[]{:S(2)}) copy-start(bf16[32,512]{1,0:T(8,128)(2,1)} %get-tuple-element.14) | copy-start | bytes 98308
